TPU v7x, 256 devices: a whole 4x4x8 slice. The times are simulated.
256 devices in a mesh: ctx: 64 (over y_lo, x, z), tp: 4 (over y_hi, core).
Axes of the slice: x: 4, y: 4 (y_hi: 2, y_lo: 2; y = y_hi * 2 + y_lo), z: 8, core: 2. Of those that a mesh axis runs over, the one named last changes fastest.
Arguments:
- tokens: bfloat16 [32768, 4096], P('ctx'), may hold values from -60 to 60
- w_query: bfloat16 [4096, 2048], P(None, 'tp'), may hold values from -0.09375 to 0.09375
- w_key: bfloat16 [4096, 512], P(None, 'tp'), may hold values from -0.09375 to 0.09375
- w_value: bfloat16 [4096, 512], P(None, 'tp'), may hold values from -0.09375 to 0.09375
- page_table: int32 [4096, 1], P('ctx'), may hold values from 0 to 63; in each aligned block of 64 rows (0 to 63, 64 to 127, ...) at most 2 rows name the same one
Outputs:
- attended: bfloat16 [32768, 2048], P('ctx', 'tp')
- kv_pool: bfloat16 [8192, 8, 2, 512], P('ctx', None, None, 'tp')
Inputs may be any that keep to these rules, and one draw needn't show every extreme that they name: `page_table`: among the 64 pages of one block at most 2 have the same owner, and some owner receives exactly 2 of them.
All inputs are finite; a program needn't handle non-finite values.
Results may differ from a plain program's by a relative error of at most 0.02.
The roundings to bfloat16 on the way count: a program that leaves them out, or rounds other values in their place, can miss the bound.
Values may be sent and summed in bfloat16 or wider, within the bound.
A program may use at most 128 MiB of HBM per device.

v0:
```python
import math

import jax
import jax.numpy as jnp
from jax import lax
from jax.sharding import PartitionSpec as P

HD = 128


theta_base = 500000.0
masked_value = -1e30


def spread(block, axis, holder):
    block = jnp.where(lax.axis_index(axis) == holder, block, jnp.zeros_like(block))
    return lax.psum(block, axis)


def rotate(projected, positions):
    row_count = projected.shape[0]
    head_count = projected.shape[1] // HD
    split_heads = projected.reshape(row_count, head_count, HD)
    half_size = HD // 2
    frequency = theta_base ** (-(jnp.arange(half_size, dtype=jnp.float32) * 2.0 / HD))
    angles = positions[:, None] * frequency[None, :]
    cosine = jnp.cos(angles)[:, None, :]
    sine_part = jnp.sin(angles)[:, None, :]
    first_half = split_heads[..., :half_size]
    second_half = split_heads[..., half_size:]
    rotated = jnp.concatenate(
        [
            first_half * cosine - second_half * sine_part,
            second_half * cosine + first_half * sine_part,
        ],
        axis=-1,
    )
    return rotated.reshape(row_count, head_count * HD)


def attend(queries, anchor_keys, anchor_values, own_keys, own_values, block_index):
    row_count = queries.shape[0]
    kv_groups = own_keys.shape[1] // HD
    group_size = queries.shape[1] // (HD * kv_groups)
    keys_all = jnp.concatenate([anchor_keys, own_keys], 0).reshape(2 * row_count, kv_groups, HD)
    values_all = jnp.concatenate([anchor_values, own_values], 0).reshape(
        2 * row_count, kv_groups, HD
    )
    query_heads = queries.reshape(row_count, kv_groups, group_size, HD)
    scores = jnp.einsum(
        "qhgd,khd->hgqk", query_heads, keys_all, preferred_element_type=jnp.float32
    ) / math.sqrt(HD)
    query_index = jnp.arange(row_count)[:, None]
    key_index = jnp.arange(2 * row_count)[None, :]
    visible = jnp.where(
        key_index < row_count, block_index > 0, key_index - row_count <= query_index
    )
    scores = jnp.where(visible, scores, masked_value)
    row_max = jnp.max(scores, axis=-1, keepdims=True)
    weights = jnp.exp(scores - row_max)
    weights = (weights / jnp.sum(weights, axis=-1, keepdims=True)).astype(jnp.bfloat16)
    mixed_heads = jnp.einsum(
        "hgqk,khd->qhgd", weights, values_all, preferred_element_type=jnp.float32
    )
    return mixed_heads.reshape(row_count, -1).astype(jnp.bfloat16)


def page_ranks(owner_table):
    page_count = owner_table.shape[1]
    page_index = jnp.arange(page_count)
    before_mask = page_index[None, :] < page_index[:, None]
    same_owner = owner_table[:, :, None] == owner_table[:, None, :]
    return jnp.sum(same_owner & before_mask[None], axis=2)


def shards(tokens, w_query, w_key, w_value, page_table):
    block_rows = tokens.shape[0]
    device = lax.axis_index("ctx")
    devices_ctx = lax.axis_size("ctx")
    positions = (device * block_rows).astype(jnp.float32) + jnp.arange(
        block_rows, dtype=jnp.float32
    )
    queries = rotate(
        jnp.dot(tokens, w_query, preferred_element_type=jnp.float32), positions
    ).astype(jnp.bfloat16)
    own_keys = rotate(jnp.dot(tokens, w_key, preferred_element_type=jnp.float32), positions).astype(
        jnp.bfloat16
    )
    own_values = jnp.dot(tokens, w_value, preferred_element_type=jnp.float32).astype(jnp.bfloat16)
    head_rows = spread(tokens, "ctx", 0)
    head_positions = jnp.arange(block_rows, dtype=jnp.float32)
    anchor_keys = rotate(
        jnp.dot(head_rows, w_key, preferred_element_type=jnp.float32), head_positions
    ).astype(jnp.bfloat16)
    anchor_values = jnp.dot(head_rows, w_value, preferred_element_type=jnp.float32).astype(
        jnp.bfloat16
    )
    attended = attend(queries, anchor_keys, anchor_values, own_keys, own_values, device)
    head_width = own_keys.shape[1]
    page_count = page_table.shape[0]
    page_length = block_rows // page_count
    kv_pages = jnp.stack(
        [
            own_keys.reshape(page_count, page_length, head_width),
            own_values.reshape(page_count, page_length, head_width),
        ],
        axis=2,
    )
    flat_pages = kv_pages.reshape(page_count, page_length * 2 * head_width)
    capacity = max(2, 2 * page_count // devices_ctx)
    slots_total = devices_ctx * capacity
    page_rank = page_ranks(page_table.reshape(1, page_count))[0]
    destination = page_table[:, 0] * capacity + page_rank
    placing = (jnp.arange(slots_total)[:, None] == destination[None, :]).astype(jnp.bfloat16)
    outgoing = jnp.dot(placing, flat_pages, preferred_element_type=jnp.float32).astype(jnp.bfloat16)
    outgoing = outgoing.reshape(slots_total, page_length, 2, head_width)
    kv_pool = lax.all_to_all(outgoing, "ctx", split_axis=0, concat_axis=0, tiled=True)
    return (attended, kv_pool)


def solution(mesh):
    return jax.shard_map(
        shards,
        mesh=mesh,
        in_specs=(P("ctx", None), P(None, "tp"), P(None, "tp"), P(None, "tp"), P("ctx", None)),
        out_specs=(P("ctx", "tp"), P("ctx", None, None, "tp")),
        check_vma=False,
    )
```

profile of v0, /device:TPU:64, one launch (start us, length us, event | category | flops | bytes accessed | tf_op | source)
XLA Modules:
  0.0 654.2 jit_solution(2168298273338521931)
XLA Ops:
  7.2 0.0 copy-start
  7.2 0.0 all-reduce.2.cloned.1.call-start
  7.2 2.3 broadcast_select_fusion
  9.5 0.0 all-reduce.2.cloned.1.call-update
  9.5 0.0 copy-done
  9.6 0.0 copy-start.3
  9.6 3.8 convolution_bitcast_fusion
  13.4 0.0 copy-start.5
  13.4 0.6 fusion.20
  14.0 0.1 copy.27
  14.1 0.0 copy-done.3
  14.1 3.4 convolution_convert_fusion.1
  17.6 0.3 copy.28
  17.8 0.2 reshape.329
  18.0 0.0 copy-done.5
  18.0 0.2 convert_reduce_fusion
  18.2 0.3 convolution_convert_fusion
  18.5 1.2 reshape.330
  19.7 12.3 %all-to-all-start = ((bf16[128,8,2,128]{3,2,1,0:T(2,128)(2,1)}), bf16[128,8,2,128]{3,2,1,0:T(2,128)(2,1)}, u32[]{:S(2)}, u32[]{:S(2)}) async-start(bf16[128,8,2,128]{3,2,1,0:T(2,128)(2,1)} %reshape.330), calls=%async_computation | async-start | bytes 1048576 | tf_op jit(solution)/shard_map/all_to_all | solution.py:117
  32.0 5.9 fusion.32
  37.9 0.1 fusion.30
  38.0 0.3 copy.36
  38.3 1.4 copy.35
  39.7 1.0 multiply_cosine_fusion
  40.7 0.8 fusion.4
  41.6 2.3 subtract_convert_fusion
  43.9 0.0 copy-start.2
  43.9 8.4 %all-to-all-done = bf16[128,8,2,128]{3,2,1,0:T(2,128)(2,1)} async-done(((bf16[128,8,2,128]{3,2,1,0:T(2,128)(2,1)}), bf16[128,8,2,128]{3,2,1,0:T(2,128)(2,1)}, u32[]{:S(2)}, u32[]{:S(2)}) %all-to-all-start) | async-done | bytes 524320 | tf_op jit(solution)/shard_map/all_to_all | solution.py:117
  52.3 579.1 %all-reduce.2.cloned.1.call-done = bf16[512,4096]{1,0:T(8,128)(2,1)} async-done(((bf16[512,4096]{1,0:T(8,128)(2,1)}), bf16[512,4096]{1,0:T(8,128)(2,1)}) %all-reduce.2.cloned.1.call-update) | async-done | bytes 4194320 | tf_op jit(solution)/shard_map/psum | solution.py:17
  631.4 3.7 convolution_bitcast_fusion.1
  635.1 0.6 subtract_convert_fusion.1
  635.7 0.0 copy-done.2
  635.7 2.0 fusion.1
  637.7 0.0 copy-start.1
  637.7 0.0 copy-start.4
  637.7 1.8 fusion
  639.6 0.3 copy-done.1
  639.9 0.3 copy-done.4
  640.2 1.3 convolution_convert_fusion.2
  641.4 2.7 fusion.5
  644.2 1.0 copy.29
  645.2 2.2 copy.39
  (9 shorter events, 0.1 us)
Async XLA Ops:
  7.2 2.4 copy-start
  7.2 624.2 %all-reduce.2.cloned.1.call-start = ((), (), s32[]{:S(2)}) async-start(), calls=%async_computation.1 | async-start | bytes 8388608 | tf_op jit(solution)/shard_map/psum | solution.py:17
  9.6 4.5 copy-start.3
  13.4 4.7 copy-start.5
  19.7 32.6 %all-to-all-start = ((bf16[128,8,2,128]{3,2,1,0:T(2,128)(2,1)}), bf16[128,8,2,128]{3,2,1,0:T(2,128)(2,1)}, u32[]{:S(2)}, u32[]{:S(2)}) async-start(bf16[128,8,2,128]{3,2,1,0:T(2,128)(2,1)} %reshape.330), calls=%async_computation | async-start | bytes 1048576 | tf_op jit(solution)/shard_map/all_to_all | solution.py:117
  43.9 591.8 %copy-start.2 = (bf16[512,4,64]{2,0,1:T(8,128)(2,1)S(1)}, bf16[512,4,64]{2,0,1:T(8,128)(2,1)}, u32[]{:S(2)}) copy-start(bf16[512,4,64]{2,0,1:T(8,128)(2,1)} %get-tuple-element.9) | copy-start | bytes 786436
  637.7 2.2 copy-start.1
  637.7 2.5 copy-start.4
Sparse Core Ops, SparseCore 0:
  10.6 620.7 all-reduce.1
where the time goes:
time: 657 us; the launch traced here: 654 us
  waiting for transfers between devices  588 us (89%)
  matrix products  23 us (4%)
  between operations  14.3 us (2%)
  starting transfers between devices  12.4 us (2%)
  other arithmetic  9.65 us (1%)
  local copies, waits for them, and re-layouts  7.36 us (1%)
    psum x1, waiting for transfers between devices, spread(): return lax.psum(block, axis)  579 us
  transfers between devices with their start and end apart: 2, of which 2 were waited for; matrix products, arithmetic and copies ran while one was open for 3% of the time, Pallas kernels for 0%

commit v1 on v0

v1 whole, which is shorter than its diff:
```python
import functools
import math

import jax
import jax.numpy as jnp
import numpy as np
from jax import lax
from jax.experimental import pallas as pl
from jax.experimental.pallas import tpu as pltpu
from jax.sharding import PartitionSpec as P

MESH = pl.DeviceIdType.MESH
HD = 128
BLK = 512
NPAGE = 64
PAGE = 8
CAP = 2
NZ = 8
THETA = 500000.0
SCALE = math.log2(math.e) / math.sqrt(HD)
F32 = jnp.float32
BF16 = jnp.bfloat16


def rope_tables(blocks):
    freq = THETA ** (-(np.arange(HD // 2, dtype=np.float64) * 2.0 / HD))
    freq = np.concatenate([freq, freq])
    sign = np.concatenate([-np.ones(HD // 2), np.ones(HD // 2)])
    rows = []
    for count, step in ((blocks, BLK), (BLK // 8, 8), (8, 1)):
        angle = np.arange(count)[:, None] * step * freq[None, :]
        rows += [np.cos(angle), np.sin(angle) * sign]
    return np.concatenate(rows, 0).astype(np.float32)


def kernel(
    n, chunks,
    tokens, w_query, w_key, w_value, owners, table,
    attended, pool,
    tok, wq, wkv, own, tab, placing, cosv, sinv, acc_kv, key_f, value_f, acc_q, pages, outgoing, kb, vb, qb, accl, row_max, anchor, va,
    small_sem, tok_sem, wk_sem, wv_sem, wq_sem, send_sem, recv_sem, step1_sem, step3_sem, a_sem, b_sem,
):
    me = lax.axis_index("ctx")
    z = lax.rem(me, NZ)
    q = lax.div(me, NZ)
    planes = n // NZ
    depth = tok.shape[2]
    rows = CAP * PAGE * 2

    own_copy = pltpu.make_async_copy(owners, own, small_sem.at[0])
    tab_copy = pltpu.make_async_copy(table, tab, small_sem.at[1])
    own_copy.start()
    tab_copy.start()

    def loads(i):
        k = pl.ds(pl.multiple_of(i * depth, depth), depth)
        return (
            pltpu.make_async_copy(w_key.at[k], wkv.at[i, :, pl.ds(0, HD)], wk_sem.at[i]),
            pltpu.make_async_copy(w_value.at[k], wkv.at[i, :, pl.ds(HD, HD)], wv_sem.at[i]),
            pltpu.make_async_copy(tokens.at[:, k], tok.at[i], tok_sem.at[i]),
        )

    def load_q(i):
        k = pl.ds(pl.multiple_of(i * depth, depth), depth)
        return pltpu.make_async_copy(w_query.at[k], wq.at[i], wq_sem.at[i])

    def start_loads(i, _):
        for copy in loads(i):
            copy.start()
        return 0

    def start_load_q(i, _):
        load_q(i).start()
        return 0

    lax.fori_loop(0, chunks, start_loads, 0)
    lax.fori_loop(0, chunks, start_load_q, 0)

    barrier = pltpu.get_barrier_semaphore()

    def greet(i, _):
        pl.semaphore_signal(barrier, inc=1, device_id={"ctx": lax.rem(me + i, n)}, device_id_type=MESH)
        return 0

    lax.fori_loop(1, n, greet, 0)

    own_copy.wait()
    tab_copy.wait()
    row_id = lax.broadcasted_iota(jnp.int32, (NPAGE, NPAGE), 0)
    col_id = lax.broadcasted_iota(jnp.int32, (NPAGE, NPAGE), 1)
    owner_row = own[...]
    owner_col = jnp.sum(jnp.where(row_id == col_id, owner_row, 0), axis=1, keepdims=True)
    rank = jnp.sum(jnp.where((owner_row == owner_col) & (row_id < col_id), 1, 0), axis=0, keepdims=True)
    slots = n * CAP
    slot_id = lax.broadcasted_iota(jnp.int32, (slots, NPAGE), 0)
    placing[...] = jnp.where(owner_row * CAP + rank == slot_id, 1.0, 0.0).astype(BF16)

    c1, s1 = tab[pl.ds(me, 1)], tab[pl.ds(n + me, 1)]
    base = 2 * n
    c2, s2 = tab[base : base + BLK // 8], tab[base + BLK // 8 : base + BLK // 4]
    base += BLK // 4
    c3, s3 = tab[base : base + 8], tab[base + 8 : base + 16]
    c12 = (c1 * c2 - s1 * s2).reshape(BLK // 8, 1, HD)
    s12 = (s1 * c2 + c1 * s2).reshape(BLK // 8, 1, HD)
    c3, s3 = c3.reshape(1, 8, HD), s3.reshape(1, 8, HD)
    cosv[...] = (c12 * c3 - s12 * s3).reshape(BLK, HD)
    sinv[...] = (s12 * c3 + c12 * s3).reshape(BLK, HD)
    vb[:, HD:] = jnp.ones((BLK, HD), BF16)
    va[:, HD:] = jnp.ones((BLK, HD), BF16)

    def rope(x):
        return x * cosv[...] + pltpu.roll(x, HD // 2, 1) * sinv[...]

    acc_kv[...] = jnp.zeros_like(acc_kv)

    def project_kv(i, _):
        for copy in loads(i):
            copy.wait()
        acc_kv[...] += jnp.dot(tok[i], wkv[i], preferred_element_type=F32)
        return 0

    lax.fori_loop(0, chunks, project_kv, 0)
    keys = rope(acc_kv[:, :HD])
    key_f[...] = keys
    value_f[...] = acc_kv[:, HD:]
    for t in range(PAGE):
        page_rows = pl.ds(t, NPAGE, stride=PAGE)
        part = jnp.concatenate([key_f[page_rows], value_f[page_rows]], axis=1).astype(BF16)
        placed = jnp.dot(placing[...], part, preferred_element_type=F32)
        pages[pl.ds(2 * t, slots, stride=2 * PAGE)] = placed[:, :HD]
        pages[pl.ds(2 * t + 1, slots, stride=2 * PAGE)] = placed[:, HD:]
    outgoing[...] = pages[...].astype(BF16)
    kb[...] = keys.astype(BF16)
    vb[:, :HD] = acc_kv[:, HD:].astype(BF16)

    def piece(k):
        return anchor.at[:, pl.ds(pl.multiple_of(k * (BLK // planes), BLK // planes), BLK // planes)]

    def send_piece(k, target, sems, i, recv):
        pltpu.make_async_remote_copy(
            src_ref=piece(k), dst_ref=piece(k), send_sem=sems.at[i], recv_sem=recv,
            device_id={"ctx": target}, device_id_type=MESH,
        ).start()

    pl.semaphore_wait(barrier, n - 1)

    @pl.when(me == 0)
    def _():
        anchor[0] = kb[...]
        anchor[1] = vb[:, :HD]

        def give(k, _):
            send_piece(k, k * NZ, step1_sem, k - 1, a_sem)
            return 0

        lax.fori_loop(1, planes, give, 0)

    def send_pages(i, _):
        owner = lax.rem(me + i, n)
        pltpu.make_async_remote_copy(
            src_ref=outgoing.at[pl.ds(pl.multiple_of(owner * rows, rows), rows)],
            dst_ref=pool.at[pl.ds(pl.multiple_of(me * rows, rows), rows)],
            send_sem=send_sem, recv_sem=recv_sem, device_id={"ctx": owner}, device_id_type=MESH,
        ).start()
        return 0

    lax.fori_loop(1, n, send_pages, 0)
    mine = pl.ds(pl.multiple_of(me * rows, rows), rows)
    pool[mine] = outgoing[mine]

    acc_q[...] = jnp.zeros_like(acc_q)

    def project_q(i, _):
        load_q(i).wait()
        acc_q[...] += jnp.dot(tok[i], wq[i], preferred_element_type=F32)
        return 0

    lax.fori_loop(0, chunks, project_q, 0)
    heads = acc_q.shape[1] // HD
    for h in range(heads):
        qb[h] = rope(acc_q[:, h * HD : (h + 1) * HD]).astype(BF16)

    @pl.when(me != 0)
    def _():
        pltpu.make_async_copy(piece(0), piece(0), a_sem).wait()

    @pl.when(z == 0)
    def _():
        def down(t, _):
            send_piece(q, q * NZ + t, step1_sem, planes - 1 + t - 1, a_sem)
            return 0

        lax.fori_loop(1, NZ, down, 0)

    def across(k, _):
        target = lax.rem(q + k, planes) * NZ + z

        @pl.when(target != 0)
        def _():
            send_piece(q, target, step3_sem, k - 1, b_sem)

        return 0

    lax.fori_loop(1, planes, across, 0)

    rb = BLK // 2
    nt = (((1,), (1,)), ((), ()))

    def own_part(h, _):
        for r in range(BLK // rb):
            lo, hi = r * rb, (r + 1) * rb
            s = lax.dot_general(qb[h, lo:hi], kb[:hi], nt, preferred_element_type=F32)
            query_id = lax.broadcasted_iota(jnp.int32, (rb, hi), 0) + lo
            key_id = lax.broadcasted_iota(jnp.int32, (rb, hi), 1)
            s = jnp.where(key_id <= query_id, s, -1e30)
            m = jnp.max(s, axis=1, keepdims=True)
            p = jnp.exp2((s - m) * SCALE).astype(BF16)
            accl[h, lo:hi] = jnp.dot(p, vb[:hi], preferred_element_type=F32)
            row_max[h, lo:hi] = jnp.broadcast_to(m, (rb, HD))
        return 0

    lax.fori_loop(0, heads, own_part, 0)

    @pl.when(me != 0)
    def _():
        rest = BLK - BLK // planes
        arrived = anchor.at[:, pl.ds(0, rest)]
        pltpu.make_async_copy(arrived, arrived, b_sem).wait()
        va[:, :HD] = anchor[1]

        def anchor_part(h, _):
            for r in range(BLK // rb):
                lo, hi = r * rb, (r + 1) * rb
                s = lax.dot_general(qb[h, lo:hi], anchor[0], nt, preferred_element_type=F32)
                before = row_max[h, lo:hi]
                m = jnp.maximum(before[:, :1], jnp.max(s, axis=1, keepdims=True))
                p = jnp.exp2((s - m) * SCALE).astype(BF16)
                keep = jnp.exp2((before - m) * SCALE)
                total = jnp.dot(p, va[...], preferred_element_type=F32)
                accl[h, lo:hi, :HD] = accl[h, lo:hi, :HD] * keep + total[:, :HD]
                accl[h, lo:hi, HD:] = accl[h, lo:hi, HD:] * keep + total[:, HD:]
            return 0

        lax.fori_loop(0, heads, anchor_part, 0)

    for h in range(heads):
        attended[:, h * HD : (h + 1) * HD] = (accl[h, :, :HD] / accl[h, :, HD:]).astype(BF16)

    def sent(sems, i):
        pltpu.make_async_copy(piece(0), piece(0), sems.at[i]).wait()

    @pl.when(me == 0)
    def _():
        def end(k, _):
            sent(step1_sem, k - 1)
            return 0

        lax.fori_loop(1, planes, end, 0)

    @pl.when(z == 0)
    def _():
        def end(t, _):
            sent(step1_sem, planes - 1 + t - 1)
            return 0

        lax.fori_loop(1, NZ, end, 0)

    def end3(k, _):
        @pl.when(lax.rem(q + k, planes) * NZ + z != 0)
        def _():
            sent(step3_sem, k - 1)

        return 0

    lax.fori_loop(1, planes, end3, 0)
    others = pool.at[pl.ds(0, (n - 1) * rows)]
    pltpu.make_async_copy(others, others, send_sem).wait()
    pltpu.make_async_copy(others, others, recv_sem).wait()


def hand_over(attended, pool, attended_out, pool_out, sem):
    copies = [
        pltpu.make_async_copy(attended, attended_out, sem.at[0]),
        pltpu.make_async_copy(pool, pool_out, sem.at[1]),
    ]
    for copy in copies:
        copy.start()
    for copy in copies:
        copy.wait()


def solution(mesh):
    n = mesh.shape["ctx"]
    table = rope_tables(n)

    def shards(tokens, w_query, w_key, w_value, page_table):
        width, heads = tokens.shape[1], w_query.shape[1] // HD
        chunks = 8
        depth = width // chunks
        hbm = pl.BlockSpec(memory_space=pltpu.HBM)
        vmem = pl.BlockSpec(memory_space=pltpu.VMEM)
        planes = n // NZ
        dma = pltpu.SemaphoreType.DMA
        operands = (tokens, w_query, w_key, w_value, page_table.reshape(1, NPAGE), jnp.asarray(table))
        attended, pool = pl.pallas_call(
            functools.partial(kernel, n, chunks),
            out_shape=(
                pltpu.VMEM((BLK, heads * HD), BF16),
                pltpu.VMEM((n * CAP * PAGE * 2, HD), BF16),
            ),
            in_specs=[hbm] * 6,
            out_specs=(vmem, vmem),
            scratch_shapes=[
                pltpu.VMEM((chunks, BLK, depth), BF16),
                pltpu.VMEM((chunks, depth, heads * HD), BF16),
                pltpu.VMEM((chunks, depth, 2 * HD), BF16),
                pltpu.VMEM((1, NPAGE), jnp.int32),
                pltpu.VMEM(table.shape, F32),
                pltpu.VMEM((n * CAP, NPAGE), BF16),
                pltpu.VMEM((BLK, HD), F32),
                pltpu.VMEM((BLK, HD), F32),
                pltpu.VMEM((BLK, 2 * HD), F32),
                pltpu.VMEM((BLK, HD), F32),
                pltpu.VMEM((BLK, HD), F32),
                pltpu.VMEM((BLK, heads * HD), F32),
                pltpu.VMEM((n * CAP * PAGE * 2, HD), F32),
                pltpu.VMEM((n * CAP * PAGE * 2, HD), BF16),
                pltpu.VMEM((BLK, HD), BF16),
                pltpu.VMEM((BLK, 2 * HD), BF16),
                pltpu.VMEM((heads, BLK, HD), BF16),
                pltpu.VMEM((heads, BLK, 2 * HD), F32),
                pltpu.VMEM((heads, BLK, HD), F32),
                pltpu.VMEM((2, BLK, HD), BF16),
                pltpu.VMEM((BLK, 2 * HD), BF16),
                dma((2,)),
                dma((chunks,)),
                dma((chunks,)),
                dma((chunks,)),
                dma((chunks,)),
                dma,
                dma,
                dma((planes - 1 + NZ - 1,)),
                dma((planes - 1,)),
                dma,
                dma,
            ],
            compiler_params=pltpu.CompilerParams(
                collective_id=0, has_side_effects=True, vmem_limit_bytes=48 << 20
            ),
        )(*[pltpu.with_memory_space_constraint(x, pltpu.HBM) for x in operands])
        attended, pool = pl.pallas_call(
            hand_over,
            out_shape=tuple(jax.ShapeDtypeStruct(x.shape, x.dtype) for x in (attended, pool)),
            in_specs=[vmem] * 2,
            out_specs=(hbm, hbm),
            scratch_shapes=[dma((2,))],
        )(*[pltpu.with_memory_space_constraint(x, pltpu.VMEM) for x in (attended, pool)])
        return attended, pool.reshape(n * CAP, PAGE, 2, HD)

    return jax.shard_map(
        shards,
        mesh=mesh,
        in_specs=(P("ctx", None), P(None, "tp"), P(None, "tp"), P(None, "tp"), P("ctx", None)),
        out_specs=(P("ctx", "tp"), P("ctx", None, None, "tp")),
        check_vma=False,
    )
```

time: 657 us -> 35.3 us (0.05)
  waiting for transfers between devices: 588 us -> 0 us
  Pallas kernels: 0 us -> 34.6 us
  matrix products: 23 us -> 0 us
  between operations: 14.3 us -> 0.64 us
  starting transfers between devices: 12.4 us -> 0 us
  other arithmetic: 9.65 us -> 0 us
  local copies, waits for them, and re-layouts: 7.36 us -> 0 us
    psum x1 -> x0, waiting for transfers between devices: 579 us -> none  [spread(): return lax.psum(block, axis)]
    pallas_call x0 -> x2, Pallas kernels: none -> 34.6 us  [the longest x1 33.6 us: shards(): pl.pallas_call(functools.partial(kernel, n, chunks), out_shape=(pltpu.VME...]
    dot_general x8 -> x0, matrix products: 23 us -> none  [the longest x1 5.86 us: shards(): jnp.dot(tokens, w_query, preferred_element_type=jnp.float32)]
    all_to_all x1 -> x0, starting transfers between devices: 12.3 us -> none  [shards(): lax.all_to_all(outgoing, 'ctx', split_axis=0, concat_axis=0, tiled=True)]
    all_to_all x1 -> x0, waiting for transfers between devices: 8.4 us -> none  [shards(): lax.all_to_all(outgoing, 'ctx', split_axis=0, concat_axis=0, tiled=True)]
  transfers between devices with their start and end apart: 2 -> 0, of which waited for: 2 -> 0; matrix products, arithmetic and copies ran while one was open for 3% -> 0% of each run, Pallas kernels for 0% -> 0%
where the time goes in v1:
time: 35.3 us; the launch traced here: 35.2 us
  Pallas kernels  34.6 us (98%)
  between operations  0.64 us (2%)
    pallas_call x1, Pallas kernels, shards(): pl.pallas_call(functools.partial(kernel, n, chunks), out_shape=(pltpu.VME...  33.6 us
    pallas_call x1, Pallas kernels, shards(): pl.pallas_call(hand_over, out_shape=tuple((jax.ShapeDtypeStruct(x.shape,...  0.99 us

profile of v1, /device:TPU:64, one launch (start us, length us, event | category | flops | bytes accessed | tf_op | source)
XLA Modules:
  0.0 35.2 jit_solution(8093531398453853129)
XLA Ops:
  0.6 33.6 %shard_map.77 = (bf16[512,512]{1,0:T(8,128)(2,1)S(1)}, bf16[2048,128]{1,0:T(8,128)(2,1)S(1)}) custom-call(bf16[512,4096]{1,0:T(8,128)(2,1)} %tokens.1, bf16[4096,512]{1,0:T(8,128)(2,1)} %w_query.1, bf16[4096,128]{1,0:T(8,128)(2,1)} %w_key.1, bf16[4096,128]{1,0:T(8,128)(2,1)} %w_value.1, s32[1,64]{1,0:T(1,128)} %bitcast.2, f32[272,128]{1,0:T(8,128)} %constant.2.clone.table), custom_call_target="tpu_custom_call" | custom-call | tf_op jit(solution)/shard_map/pallas_call | solution.py:305
  34.2 1.0 %shard_map.78 = (bf16[512,512]{1,0:T(8,128)(2,1)}, bf16[2048,128]{1,0:T(8,128)(2,1)}) custom-call(bf16[512,512]{1,0:T(8,128)(2,1)S(1)} %get-tuple-element.6.attended, bf16[2048,128]{1,0:T(8,128)(2,1)S(1)} %get-tuple-element.7.pool), custom_call_target="tpu_custom_call" | custom-call | tf_op jit(solution)/shard_map/pallas_call | solution.py:351

commit v2 on v1

--- a/solution.py
+++ b/solution.py
@@ -16,6 +16,7 @@
 PAGE = 8
 CAP = 2
 NZ = 8
+EARLY = 4
 THETA = 500000.0
 SCALE = math.log2(math.e) / math.sqrt(HD)
 F32 = jnp.float32
@@ -34,17 +35,16 @@
 
 
 def kernel(
-    n, chunks,
+    n,
     tokens, w_query, w_key, w_value, owners, table,
     attended, pool,
     tok, wq, wkv, own, tab, placing, cosv, sinv, acc_kv, key_f, value_f, acc_q, pages, outgoing, kb, vb, qb, accl, row_max, anchor, va,
-    small_sem, tok_sem, wk_sem, wv_sem, wq_sem, send_sem, recv_sem, step1_sem, step3_sem, a_sem, b_sem,
+    small_sem, load_sem, send_sem, recv_sem, step1_sem, step3_sem, a_sem, b_sem, here_sem, count_sem, early_sem, go_sem,
 ):
     me = lax.axis_index("ctx")
     z = lax.rem(me, NZ)
     q = lax.div(me, NZ)
     planes = n // NZ
-    depth = tok.shape[2]
     rows = CAP * PAGE * 2
 
     own_copy = pltpu.make_async_copy(owners, own, small_sem.at[0])
@@ -52,37 +52,44 @@
     own_copy.start()
     tab_copy.start()
 
-    def loads(i):
-        k = pl.ds(pl.multiple_of(i * depth, depth), depth)
-        return (
-            pltpu.make_async_copy(w_key.at[k], wkv.at[i, :, pl.ds(0, HD)], wk_sem.at[i]),
-            pltpu.make_async_copy(w_value.at[k], wkv.at[i, :, pl.ds(HD, HD)], wv_sem.at[i]),
-            pltpu.make_async_copy(tokens.at[:, k], tok.at[i], tok_sem.at[i]),
-        )
-
-    def load_q(i):
-        k = pl.ds(pl.multiple_of(i * depth, depth), depth)
-        return pltpu.make_async_copy(w_query.at[k], wq.at[i], wq_sem.at[i])
-
-    def start_loads(i, _):
-        for copy in loads(i):
-            copy.start()
-        return 0
-
-    def start_load_q(i, _):
-        load_q(i).start()
-        return 0
-
-    lax.fori_loop(0, chunks, start_loads, 0)
-    lax.fori_loop(0, chunks, start_load_q, 0)
+    loads = (
+        pltpu.make_async_copy(w_key, wkv.at[:, pl.ds(0, HD)], load_sem.at[0]),
+        pltpu.make_async_copy(w_value, wkv.at[:, pl.ds(HD, HD)], load_sem.at[1]),
+        pltpu.make_async_copy(tokens, tok, load_sem.at[2]),
+    )
+    load_q = pltpu.make_async_copy(w_query, wq, load_sem.at[3])
+    for copy in loads:
+        copy.start()
 
     barrier = pltpu.get_barrier_semaphore()
 
-    def greet(i, _):
-        pl.semaphore_signal(barrier, inc=1, device_id={"ctx": lax.rem(me + i, n)}, device_id_type=MESH)
-        return 0
-
-    lax.fori_loop(1, n, greet, 0)
+    def tell(sem, target):
+        pl.semaphore_signal(sem, inc=1, device_id={"ctx": target}, device_id_type=MESH)
+
+    def tell_mates(sem):
+        def one(k, _):
+            tell(sem, lax.rem(q + k, planes) * NZ + z)
+            return 0
+
+        lax.fori_loop(1, planes, one, 0)
+
+    def tell_column(sem, lo, hi):
+        def one(t, _):
+            tell(sem, q * NZ + t)
+            return 0
+
+        lax.fori_loop(lo, hi, one, 0)
+
+    @pl.when(z == 0)
+    def _():
+        tell_mates(barrier)
+        pl.semaphore_wait(barrier, planes - 1)
+        tell_column(barrier, 1, NZ)
+
+    @pl.when(z != 0)
+    def _():
+        pl.semaphore_wait(barrier, 1)
+        tell(here_sem.at[z], q * NZ)
 
     own_copy.wait()
     tab_copy.wait()
@@ -111,16 +118,34 @@
     def rope(x):
         return x * cosv[...] + pltpu.roll(x, HD // 2, 1) * sinv[...]
 
-    acc_kv[...] = jnp.zeros_like(acc_kv)
-
-    def project_kv(i, _):
-        for copy in loads(i):
-            copy.wait()
-        acc_kv[...] += jnp.dot(tok[i], wkv[i], preferred_element_type=F32)
-        return 0
-
-    lax.fori_loop(0, chunks, project_kv, 0)
+    for copy in loads:
+        copy.wait()
+    load_q.start()
+    acc_kv[...] = jnp.dot(tok[...], wkv[...], preferred_element_type=F32)
     keys = rope(acc_kv[:, :HD])
+    kb[...] = keys.astype(BF16)
+    vb[:, :HD] = acc_kv[:, HD:].astype(BF16)
+
+    def piece(k):
+        return anchor.at[:, pl.ds(pl.multiple_of(k * (BLK // planes), BLK // planes), BLK // planes)]
+
+    def send_piece(k, target, sems, i, recv):
+        pltpu.make_async_remote_copy(
+            src_ref=piece(k), dst_ref=piece(k), send_sem=sems.at[i], recv_sem=recv,
+            device_id={"ctx": target}, device_id_type=MESH,
+        ).start()
+
+    @pl.when(me == 0)
+    def _():
+        anchor[0] = kb[...]
+        anchor[1] = vb[:, :HD]
+
+        def give(k, _):
+            send_piece(k, k * NZ, step1_sem, k - 1, a_sem)
+            return 0
+
+        lax.fori_loop(1, planes, give, 0)
+
     key_f[...] = keys
     value_f[...] = acc_kv[:, HD:]
     for t in range(PAGE):
@@ -130,84 +155,106 @@
         pages[pl.ds(2 * t, slots, stride=2 * PAGE)] = placed[:, :HD]
         pages[pl.ds(2 * t + 1, slots, stride=2 * PAGE)] = placed[:, HD:]
     outgoing[...] = pages[...].astype(BF16)
-    kb[...] = keys.astype(BF16)
-    vb[:, :HD] = acc_kv[:, HD:].astype(BF16)
-
-    def piece(k):
-        return anchor.at[:, pl.ds(pl.multiple_of(k * (BLK // planes), BLK // planes), BLK // planes)]
-
-    def send_piece(k, target, sems, i, recv):
-        pltpu.make_async_remote_copy(
-            src_ref=piece(k), dst_ref=piece(k), send_sem=sems.at[i], recv_sem=recv,
-            device_id={"ctx": target}, device_id_type=MESH,
-        ).start()
-
-    pl.semaphore_wait(barrier, n - 1)
-
-    @pl.when(me == 0)
-    def _():
-        anchor[0] = kb[...]
-        anchor[1] = vb[:, :HD]
-
-        def give(k, _):
-            send_piece(k, k * NZ, step1_sem, k - 1, a_sem)
-            return 0
-
-        lax.fori_loop(1, planes, give, 0)
-
-    def send_pages(i, _):
-        owner = lax.rem(me + i, n)
-        pltpu.make_async_remote_copy(
-            src_ref=outgoing.at[pl.ds(pl.multiple_of(owner * rows, rows), rows)],
-            dst_ref=pool.at[pl.ds(pl.multiple_of(me * rows, rows), rows)],
-            send_sem=send_sem, recv_sem=recv_sem, device_id={"ctx": owner}, device_id_type=MESH,
-        ).start()
-        return 0
-
-    lax.fori_loop(1, n, send_pages, 0)
+
     mine = pl.ds(pl.multiple_of(me * rows, rows), rows)
     pool[mine] = outgoing[mine]
 
-    acc_q[...] = jnp.zeros_like(acc_q)
-
-    def project_q(i, _):
-        load_q(i).wait()
-        acc_q[...] += jnp.dot(tok[i], wq[i], preferred_element_type=F32)
+    def send_column(j, first, count):
+        def one(t, _):
+            owner = lax.rem(q + j, planes) * NZ + first + lax.rem(z + t, count)
+
+            @pl.when(owner != me)
+            def _():
+                pltpu.make_async_remote_copy(
+                    src_ref=outgoing.at[pl.ds(pl.multiple_of(owner * rows, rows), rows)],
+                    dst_ref=pool.at[mine],
+                    send_sem=send_sem, recv_sem=recv_sem, device_id={"ctx": owner}, device_id_type=MESH,
+                ).start()
+
+            return 0
+
+        lax.fori_loop(0, count, one, 0)
+
+    def send_planes(first, count):
+        def one(j, _):
+            send_column(j, first, count)
+            return 0
+
+        lax.fori_loop(0, planes, one, 0)
+
+    def wait_piece():
+        pltpu.make_async_copy(piece(0), piece(0), a_sem).wait()
+
+    def give_mate(k):
+        target = lax.rem(q + k, planes) * NZ + z
+
+        @pl.when(target != 0)
+        def _():
+            send_piece(q, target, step3_sem, k - 1, b_sem)
+
+    def share():
+        def across(k, _):
+            give_mate(k)
+            return 0
+
+        lax.fori_loop(1, planes, across, 0)
+
+    def see(t, _):
+        pl.semaphore_wait(here_sem.at[t], 1)
         return 0
 
-    lax.fori_loop(0, chunks, project_q, 0)
+    def down(t, _):
+        send_piece(q, q * NZ + t, step1_sem, planes - 1 + t - 1, a_sem)
+        return 0
+
+    @pl.when(z >= EARLY)
+    def _():
+        send_planes(0, 1)
+        pl.semaphore_wait(go_sem, 1)
+        send_planes(1, NZ - 1)
+
+    @pl.when((z > 0) & (z < EARLY))
+    def _():
+        pl.semaphore_wait(early_sem, 1)
+        send_planes(0, EARLY)
+
+    @pl.when(z == 0)
+    def _():
+        lax.fori_loop(1, EARLY, see, 0)
+        tell_mates(count_sem.at[0])
+        pl.semaphore_wait(count_sem.at[0], planes - 1)
+        tell_column(early_sem, 1, EARLY)
+        lax.fori_loop(EARLY, NZ, see, 0)
+        tell_mates(count_sem.at[1])
+        pl.semaphore_wait(count_sem.at[1], planes - 1)
+        tell_column(go_sem, 1, NZ)
+
+        @pl.when(me != 0)
+        def _():
+            wait_piece()
+
+        lax.fori_loop(1, NZ, down, 0)
+        share()
+        send_planes(0, NZ)
+
+    load_q.wait()
+    acc_q[...] = jnp.dot(tok[...], wq[...], preferred_element_type=F32)
     heads = acc_q.shape[1] // HD
     for h in range(heads):
         qb[h] = rope(acc_q[:, h * HD : (h + 1) * HD]).astype(BF16)
 
-    @pl.when(me != 0)
-    def _():
-        pltpu.make_async_copy(piece(0), piece(0), a_sem).wait()
-
-    @pl.when(z == 0)
-    def _():
-        def down(t, _):
-            send_piece(q, q * NZ + t, step1_sem, planes - 1 + t - 1, a_sem)
-            return 0
-
-        lax.fori_loop(1, NZ, down, 0)
-
-    def across(k, _):
-        target = lax.rem(q + k, planes) * NZ + z
-
-        @pl.when(target != 0)
-        def _():
-            send_piece(q, target, step3_sem, k - 1, b_sem)
-
-        return 0
-
-    lax.fori_loop(1, planes, across, 0)
+    @pl.when((z > 0) & (z < EARLY))
+    def _():
+        wait_piece()
+        share()
+        pl.semaphore_wait(go_sem, 1)
+        send_planes(EARLY, NZ - EARLY)
 
     rb = BLK // 2
     nt = (((1,), (1,)), ((), ()))
 
-    def own_part(h, _):
-        for r in range(BLK // rb):
+    def own_part(i, _):
+        for h, r in [(2 * i + j, r) for j in range(2) for r in range(BLK // rb)]:
             lo, hi = r * rb, (r + 1) * rb
             s = lax.dot_general(qb[h, lo:hi], kb[:hi], nt, preferred_element_type=F32)
             query_id = lax.broadcasted_iota(jnp.int32, (rb, hi), 0) + lo
@@ -219,7 +266,12 @@
             row_max[h, lo:hi] = jnp.broadcast_to(m, (rb, HD))
         return 0
 
-    lax.fori_loop(0, heads, own_part, 0)
+    lax.fori_loop(0, heads // 2, own_part, 0)
+
+    @pl.when(z >= EARLY)
+    def _():
+        wait_piece()
+        share()
 
     @pl.when(me != 0)
     def _():
@@ -228,8 +280,8 @@
         pltpu.make_async_copy(arrived, arrived, b_sem).wait()
         va[:, :HD] = anchor[1]
 
-        def anchor_part(h, _):
-            for r in range(BLK // rb):
+        def anchor_part(i, _):
+            for h, r in [(2 * i + j, r) for j in range(2) for r in range(BLK // rb)]:
                 lo, hi = r * rb, (r + 1) * rb
                 s = lax.dot_general(qb[h, lo:hi], anchor[0], nt, preferred_element_type=F32)
                 before = row_max[h, lo:hi]
@@ -241,7 +293,7 @@
                 accl[h, lo:hi, HD:] = accl[h, lo:hi, HD:] * keep + total[:, HD:]
             return 0
 
-        lax.fori_loop(0, heads, anchor_part, 0)
+        lax.fori_loop(0, heads // 2, anchor_part, 0)
 
     for h in range(heads):
         attended[:, h * HD : (h + 1) * HD] = (accl[h, :, :HD] / accl[h, :, HD:]).astype(BF16)
@@ -295,15 +347,13 @@
 
     def shards(tokens, w_query, w_key, w_value, page_table):
         width, heads = tokens.shape[1], w_query.shape[1] // HD
-        chunks = 8
-        depth = width // chunks
         hbm = pl.BlockSpec(memory_space=pltpu.HBM)
         vmem = pl.BlockSpec(memory_space=pltpu.VMEM)
         planes = n // NZ
         dma = pltpu.SemaphoreType.DMA
         operands = (tokens, w_query, w_key, w_value, page_table.reshape(1, NPAGE), jnp.asarray(table))
         attended, pool = pl.pallas_call(
-            functools.partial(kernel, n, chunks),
+            functools.partial(kernel, n),
             out_shape=(
                 pltpu.VMEM((BLK, heads * HD), BF16),
                 pltpu.VMEM((n * CAP * PAGE * 2, HD), BF16),
@@ -311,9 +361,9 @@
             in_specs=[hbm] * 6,
             out_specs=(vmem, vmem),
             scratch_shapes=[
-                pltpu.VMEM((chunks, BLK, depth), BF16),
-                pltpu.VMEM((chunks, depth, heads * HD), BF16),
-                pltpu.VMEM((chunks, depth, 2 * HD), BF16),
+                pltpu.VMEM((BLK, width), BF16),
+                pltpu.VMEM((width, heads * HD), BF16),
+                pltpu.VMEM((width, 2 * HD), BF16),
                 pltpu.VMEM((1, NPAGE), jnp.int32),
                 pltpu.VMEM(table.shape, F32),
                 pltpu.VMEM((n * CAP, NPAGE), BF16),
@@ -333,16 +383,17 @@
                 pltpu.VMEM((2, BLK, HD), BF16),
                 pltpu.VMEM((BLK, 2 * HD), BF16),
                 dma((2,)),
-                dma((chunks,)),
-                dma((chunks,)),
-                dma((chunks,)),
-                dma((chunks,)),
+                dma((4,)),
                 dma,
                 dma,
                 dma((planes - 1 + NZ - 1,)),
                 dma((planes - 1,)),
                 dma,
                 dma,
+                pltpu.SemaphoreType.REGULAR((NZ,)),
+                pltpu.SemaphoreType.REGULAR((2,)),
+                pltpu.SemaphoreType.REGULAR,
+                pltpu.SemaphoreType.REGULAR,
             ],
             compiler_params=pltpu.CompilerParams(
                 collective_id=0, has_side_effects=True, vmem_limit_bytes=48 << 20

time: 35.3 us -> 30.2 us (0.86)
  the two profiles are of different devices: /device:TPU:64 before, /device:TPU:224 now
where the time goes in v2:
time: 30.2 us; the launch traced here: 30.1 us
  Pallas kernels  29.4 us (97%)
  between operations  0.64 us (2%)
    pallas_call x1, Pallas kernels, shards(): pl.pallas_call(functools.partial(kernel, n), out_shape=(pltpu.VMEM((BLK,...  28.5 us
    pallas_call x1, Pallas kernels, shards(): pl.pallas_call(hand_over, out_shape=tuple((jax.ShapeDtypeStruct(x.shape,...  0.99 us

profile of v2, /device:TPU:224, one launch (start us, length us, event | category | flops | bytes accessed | tf_op | source)
XLA Modules:
  0.0 30.1 jit_solution(8809085563896424506)
XLA Ops:
  0.6 28.5 %shard_map.77 = (bf16[512,512]{1,0:T(8,128)(2,1)S(1)}, bf16[2048,128]{1,0:T(8,128)(2,1)S(1)}) custom-call(bf16[512,4096]{1,0:T(8,128)(2,1)} %tokens.1, bf16[4096,512]{1,0:T(8,128)(2,1)} %w_query.1, bf16[4096,128]{1,0:T(8,128)(2,1)} %w_key.1, bf16[4096,128]{1,0:T(8,128)(2,1)} %w_value.1, s32[1,64]{1,0:T(1,128)} %bitcast.2, f32[272,128]{1,0:T(8,128)} %constant.2.clone.table), custom_call_target="tpu_custom_call" | custom-call | tf_op jit(solution)/shard_map/pallas_call | solution.py:355
  29.1 1.0 %shard_map.78 = (bf16[512,512]{1,0:T(8,128)(2,1)}, bf16[2048,128]{1,0:T(8,128)(2,1)}) custom-call(bf16[512,512]{1,0:T(8,128)(2,1)S(1)} %get-tuple-element.6.attended, bf16[2048,128]{1,0:T(8,128)(2,1)S(1)} %get-tuple-element.7.pool), custom_call_target="tpu_custom_call" | custom-call | tf_op jit(solution)/shard_map/pallas_call | solution.py:402

commit v3 on v2

--- a/solution.py
+++ b/solution.py
@@ -203,20 +203,28 @@
         pl.semaphore_wait(here_sem.at[t], 1)
         return 0
 
+    def see_late(t, _):
+        see(t, 0)
+        tell(early_sem, q * NZ + t)
+        return 0
+
     def down(t, _):
         send_piece(q, q * NZ + t, step1_sem, planes - 1 + t - 1, a_sem)
         return 0
 
-    @pl.when(z >= EARLY)
-    def _():
-        send_planes(0, 1)
-        pl.semaphore_wait(go_sem, 1)
-        send_planes(1, NZ - 1)
-
     @pl.when((z > 0) & (z < EARLY))
     def _():
         pl.semaphore_wait(early_sem, 1)
         send_planes(0, EARLY)
+
+    @pl.when(z >= EARLY)
+    def _():
+        pl.semaphore_wait(early_sem, 1)
+        send_planes(0, 2)
+        pl.semaphore_wait(go_sem, 1)
+        wait_piece()
+        share()
+        send_planes(2, EARLY - 2)
 
     @pl.when(z == 0)
     def _():
@@ -224,16 +232,17 @@
         tell_mates(count_sem.at[0])
         pl.semaphore_wait(count_sem.at[0], planes - 1)
         tell_column(early_sem, 1, EARLY)
-        lax.fori_loop(EARLY, NZ, see, 0)
-        tell_mates(count_sem.at[1])
-        pl.semaphore_wait(count_sem.at[1], planes - 1)
-        tell_column(go_sem, 1, NZ)
 
         @pl.when(me != 0)
         def _():
             wait_piece()
 
-        lax.fori_loop(1, NZ, down, 0)
+        lax.fori_loop(1, EARLY, down, 0)
+        lax.fori_loop(EARLY, NZ, see_late, 0)
+        tell_mates(count_sem.at[1])
+        lax.fori_loop(EARLY, NZ, down, 0)
+        pl.semaphore_wait(count_sem.at[1], planes - 1)
+        tell_column(go_sem, 1, NZ)
         share()
         send_planes(0, NZ)
 
@@ -248,6 +257,10 @@
         wait_piece()
         share()
         pl.semaphore_wait(go_sem, 1)
+        send_planes(EARLY, NZ - EARLY)
+
+    @pl.when(z >= EARLY)
+    def _():
         send_planes(EARLY, NZ - EARLY)
 
     rb = BLK // 2
@@ -267,11 +280,6 @@
         return 0
 
     lax.fori_loop(0, heads // 2, own_part, 0)
-
-    @pl.when(z >= EARLY)
-    def _():
-        wait_piece()
-        share()
 
     @pl.when(me != 0)
     def _():

time: 30.2 us -> 28.2 us (0.934)
  the two profiles are of different devices: /device:TPU:224 before, /device:TPU:64 now
where the time goes in v3:
time: 28.2 us; the launch traced here: 27.8 us
  Pallas kernels  27.2 us (96%)
  between operations  0.64 us (2%)
    pallas_call x1, Pallas kernels, shards(): pl.pallas_call(functools.partial(kernel, n), out_shape=(pltpu.VMEM((BLK,...  26.2 us
    pallas_call x1, Pallas kernels, shards(): pl.pallas_call(hand_over, out_shape=tuple((jax.ShapeDtypeStruct(x.shape,...  0.99 us

profile of v3, /device:TPU:64, one launch (start us, length us, event | category | flops | bytes accessed | tf_op | source)
XLA Modules:
  0.0 27.8 jit_solution(17582531319799188175)
XLA Ops:
  0.6 26.2 %shard_map.77 = (bf16[512,512]{1,0:T(8,128)(2,1)S(1)}, bf16[2048,128]{1,0:T(8,128)(2,1)S(1)}) custom-call(bf16[512,4096]{1,0:T(8,128)(2,1)} %tokens.1, bf16[4096,512]{1,0:T(8,128)(2,1)} %w_query.1, bf16[4096,128]{1,0:T(8,128)(2,1)} %w_key.1, bf16[4096,128]{1,0:T(8,128)(2,1)} %w_value.1, s32[1,64]{1,0:T(1,128)} %bitcast.2, f32[272,128]{1,0:T(8,128)} %constant.2.clone.table), custom_call_target="tpu_custom_call" | custom-call | tf_op jit(solution)/shard_map/pallas_call | solution.py:363
  26.9 1.0 %shard_map.78 = (bf16[512,512]{1,0:T(8,128)(2,1)}, bf16[2048,128]{1,0:T(8,128)(2,1)}) custom-call(bf16[512,512]{1,0:T(8,128)(2,1)S(1)} %get-tuple-element.6.attended, bf16[2048,128]{1,0:T(8,128)(2,1)S(1)} %get-tuple-element.7.pool), custom_call_target="tpu_custom_call" | custom-call | tf_op jit(solution)/shard_map/pallas_call | solution.py:410

commit v4 on v3

--- a/solution.py
+++ b/solution.py
@@ -80,11 +80,23 @@
 
         lax.fori_loop(lo, hi, one, 0)
 
+    def see(t, _):
+        pl.semaphore_wait(here_sem.at[t], 1)
+        return 0
+
+    def see_early():
+        lax.fori_loop(1, EARLY, see, 0)
+        tell_mates(count_sem.at[0])
+
     @pl.when(z == 0)
     def _():
         tell_mates(barrier)
         pl.semaphore_wait(barrier, planes - 1)
         tell_column(barrier, 1, NZ)
+
+        @pl.when(me != 0)
+        def _():
+            see_early()
 
     @pl.when(z != 0)
     def _():
@@ -145,6 +157,7 @@
             return 0
 
         lax.fori_loop(1, planes, give, 0)
+        see_early()
 
     key_f[...] = keys
     value_f[...] = acc_kv[:, HD:]
@@ -199,10 +212,6 @@
 
         lax.fori_loop(1, planes, across, 0)
 
-    def see(t, _):
-        pl.semaphore_wait(here_sem.at[t], 1)
-        return 0
-
     def see_late(t, _):
         see(t, 0)
         tell(early_sem, q * NZ + t)
@@ -220,31 +229,30 @@
     @pl.when(z >= EARLY)
     def _():
         pl.semaphore_wait(early_sem, 1)
-        send_planes(0, 2)
+        send_planes(0, 3)
         pl.semaphore_wait(go_sem, 1)
         wait_piece()
         share()
-        send_planes(2, EARLY - 2)
+        send_planes(3, EARLY - 3)
 
     @pl.when(z == 0)
     def _():
-        lax.fori_loop(1, EARLY, see, 0)
-        tell_mates(count_sem.at[0])
         pl.semaphore_wait(count_sem.at[0], planes - 1)
         tell_column(early_sem, 1, EARLY)
+        lax.fori_loop(EARLY, NZ, see_late, 0)
+        tell_mates(count_sem.at[1])
 
         @pl.when(me != 0)
         def _():
             wait_piece()
 
+        lax.fori_loop(EARLY, NZ, lambda t, _: down(NZ - 1 + EARLY - t, 0), 0)
         lax.fori_loop(1, EARLY, down, 0)
-        lax.fori_loop(EARLY, NZ, see_late, 0)
-        tell_mates(count_sem.at[1])
-        lax.fori_loop(EARLY, NZ, down, 0)
         pl.semaphore_wait(count_sem.at[1], planes - 1)
         tell_column(go_sem, 1, NZ)
+        send_planes(EARLY, NZ - EARLY)
         share()
-        send_planes(0, NZ)
+        send_planes(0, EARLY)
 
     load_q.wait()
     acc_q[...] = jnp.dot(tok[...], wq[...], preferred_element_type=F32)
@@ -297,14 +305,21 @@
                 p = jnp.exp2((s - m) * SCALE).astype(BF16)
                 keep = jnp.exp2((before - m) * SCALE)
                 total = jnp.dot(p, va[...], preferred_element_type=F32)
-                accl[h, lo:hi, :HD] = accl[h, lo:hi, :HD] * keep + total[:, :HD]
-                accl[h, lo:hi, HD:] = accl[h, lo:hi, HD:] * keep + total[:, HD:]
+                top = accl[h, lo:hi, :HD] * keep + total[:, :HD]
+                weight = accl[h, lo:hi, HD:] * keep + total[:, HD:]
+                attended[lo:hi, pl.ds(pl.multiple_of(h * HD, HD), HD)] = (top / weight).astype(BF16)
             return 0
 
         lax.fori_loop(0, heads // 2, anchor_part, 0)
 
-    for h in range(heads):
-        attended[:, h * HD : (h + 1) * HD] = (accl[h, :, :HD] / accl[h, :, HD:]).astype(BF16)
+    @pl.when(me == 0)
+    def _():
+        def own_only(h, _):
+            out = accl[h, :, :HD] / accl[h, :, HD:]
+            attended[:, pl.ds(pl.multiple_of(h * HD, HD), HD)] = out.astype(BF16)
+            return 0
+
+        lax.fori_loop(0, heads, own_only, 0)
 
     def sent(sems, i):
         pltpu.make_async_copy(piece(0), piece(0), sems.at[i]).wait()

time: 28.2 us -> 27.4 us (0.972)
  Pallas kernels: 27.2 us -> 26.4 us
    pallas_call x1, Pallas kernels: 26.2 us -> 25.4 us  [shards(): pl.pallas_call(functools.partial(kernel, n), out_shape=(pltpu.VMEM((BLK,...]
where the time goes in v4:
time: 27.4 us; the launch traced here: 27 us
  Pallas kernels  26.4 us (96%)
  between operations  0.64 us (2%)
    pallas_call x1, Pallas kernels, shards(): pl.pallas_call(functools.partial(kernel, n), out_shape=(pltpu.VMEM((BLK,...  25.4 us
    pallas_call x1, Pallas kernels, shards(): pl.pallas_call(hand_over, out_shape=tuple((jax.ShapeDtypeStruct(x.shape,...  0.99 us

profile of v4, /device:TPU:64, one launch (start us, length us, event | category | flops | bytes accessed | tf_op | source)
XLA Modules:
  0.0 27.0 jit_solution(15163462634210880426)
XLA Ops:
  0.6 25.4 %shard_map.77 = (bf16[512,512]{1,0:T(8,128)(2,1)S(1)}, bf16[2048,128]{1,0:T(8,128)(2,1)S(1)}) custom-call(bf16[512,4096]{1,0:T(8,128)(2,1)} %tokens.1, bf16[4096,512]{1,0:T(8,128)(2,1)} %w_query.1, bf16[4096,128]{1,0:T(8,128)(2,1)} %w_key.1, bf16[4096,128]{1,0:T(8,128)(2,1)} %w_value.1, s32[1,64]{1,0:T(1,128)} %bitcast.2, f32[272,128]{1,0:T(8,128)} %constant.2.clone.table), custom_call_target="tpu_custom_call" | custom-call | tf_op jit(solution)/shard_map/pallas_call | solution.py:378
  26.0 1.0 %shard_map.78 = (bf16[512,512]{1,0:T(8,128)(2,1)}, bf16[2048,128]{1,0:T(8,128)(2,1)}) custom-call(bf16[512,512]{1,0:T(8,128)(2,1)S(1)} %get-tuple-element.6.attended, bf16[2048,128]{1,0:T(8,128)(2,1)S(1)} %get-tuple-element.7.pool), custom_call_target="tpu_custom_call" | custom-call | tf_op jit(solution)/shard_map/pallas_call | solution.py:425

commit v5 on v4

--- a/solution.py
+++ b/solution.py
@@ -262,10 +262,10 @@
 
     @pl.when((z > 0) & (z < EARLY))
     def _():
+        pl.semaphore_wait(go_sem, 1)
+        send_planes(EARLY, NZ - EARLY)
         wait_piece()
         share()
-        pl.semaphore_wait(go_sem, 1)
-        send_planes(EARLY, NZ - EARLY)
 
     @pl.when(z >= EARLY)
     def _():

time: 27.4 us -> 27.4 us (level)
  no operation moved by 1% of the time
where the time goes in v5:
time: 27.4 us; the launch traced here: 27 us
  Pallas kernels  26.4 us (96%)
  between operations  0.64 us (2%)
    pallas_call x1, Pallas kernels, shards(): pl.pallas_call(functools.partial(kernel, n), out_shape=(pltpu.VMEM((BLK,...  25.4 us
    pallas_call x1, Pallas kernels, shards(): pl.pallas_call(hand_over, out_shape=tuple((jax.ShapeDtypeStruct(x.shape,...  0.99 us

profile of v5, /device:TPU:64, one launch (start us, length us, event | category | flops | bytes accessed | tf_op | source)
XLA Modules:
  0.0 27.0 jit_solution(9894209281527177748)
XLA Ops:
  0.6 25.4 %shard_map.77 = (bf16[512,512]{1,0:T(8,128)(2,1)S(1)}, bf16[2048,128]{1,0:T(8,128)(2,1)S(1)}) custom-call(bf16[512,4096]{1,0:T(8,128)(2,1)} %tokens.1, bf16[4096,512]{1,0:T(8,128)(2,1)} %w_query.1, bf16[4096,128]{1,0:T(8,128)(2,1)} %w_key.1, bf16[4096,128]{1,0:T(8,128)(2,1)} %w_value.1, s32[1,64]{1,0:T(1,128)} %bitcast.2, f32[272,128]{1,0:T(8,128)} %constant.2.clone.table), custom_call_target="tpu_custom_call" | custom-call | tf_op jit(solution)/shard_map/pallas_call | solution.py:378
  26.0 1.0 %shard_map.78 = (bf16[512,512]{1,0:T(8,128)(2,1)}, bf16[2048,128]{1,0:T(8,128)(2,1)}) custom-call(bf16[512,512]{1,0:T(8,128)(2,1)S(1)} %get-tuple-element.6.attended, bf16[2048,128]{1,0:T(8,128)(2,1)S(1)} %get-tuple-element.7.pool), custom_call_target="tpu_custom_call" | custom-call | tf_op jit(solution)/shard_map/pallas_call | solution.py:425
